TPU v7x, 512 devices: a whole 4x4x16 slice. The times are simulated.
512 devices in a mesh: dom: 128 (over z, y_hi, x), cls: 4 (over y_lo, core).
Axes of the slice: x: 4, y: 4 (y_hi: 2, y_lo: 2; y = y_hi * 2 + y_lo), z: 16, core: 2. Of those that a mesh axis runs over, the one named last changes fastest.
Arguments:
- particles: float32 [1024, 64, 256], P('dom'), may hold values from -64 to 64
- references: float32 [128, 16384], P('cls', 'dom'), may hold values from -1 to 1
- noise_var: float32 [64], replicated, may hold values from 0.4 to 2.5
Outputs:
- averages: float32 [128, 16384], P('cls', 'dom')
- noise_new: float32 [64], replicated
- evidence: float32 [1024], P('dom')
All inputs are finite; a program needn't handle non-finite values.
Results may differ from a plain program's by a relative error of at most 0.0003.
Values sent between devices are 32-bit elements; how exact they have to be, the bound alone decides.
No kernel may reach another device: no remote copies, remote signals or barrier semaphores. Data moves between devices by JAX's collectives and lax.ppermute only.
A program may use at most 64 MiB of HBM per device.

v0:
```python
import math

import jax
import jax.numpy as jnp
from jax import lax
from jax.sharding import PartitionSpec as P

highest = lax.Precision.HIGHEST


def angle_tables(length):
    middle = length // 2
    angle_index = jnp.arange(length, dtype=jnp.int32)
    slot_index = jnp.arange(middle, dtype=jnp.int32)
    phase_index = angle_index[:, None] * slot_index[None, :] % length
    radians = phase_index.astype(jnp.float32) * (2.0 * math.pi / length)
    cosine = jnp.cos(radians)
    sine_table = jnp.sin(radians)
    alternate = jnp.where(angle_index % 2 == 0, 1.0, -1.0).astype(jnp.float32)
    leading = slot_index == 0
    forward = jnp.concatenate(
        [cosine, jnp.where(leading[None, :], alternate[:, None], -sine_table)], axis=1
    )
    slot_weight = jnp.where(leading, 1.0, 2.0).astype(jnp.float32) / length
    inverse_real = cosine.T * slot_weight[:, None]
    inverse_imag = jnp.where(
        leading[:, None], alternate[None, :] / length, -2.0 * sine_table.T / length
    )
    inverse = jnp.concatenate([inverse_real, inverse_imag], axis=0)
    parseval = jnp.concatenate([slot_weight, slot_weight])
    return (forward, inverse, parseval)


def conj_product(left_re, left_im, right_re, right_im, pattern):
    real_real = jnp.einsum(pattern, left_re, right_re, precision=highest)
    imag_imag = jnp.einsum(pattern, left_im, right_im, precision=highest)
    imag_real = jnp.einsum(pattern, left_im, right_re, precision=highest)
    real_imag = jnp.einsum(pattern, left_re, right_im, precision=highest)
    leading = jnp.arange(real_real.shape[-1]) == 0
    real_part = real_real + jnp.where(leading, 0.0, imag_imag)
    imag_part = jnp.where(leading, imag_imag, imag_real - real_imag)
    return jnp.concatenate([real_part, imag_part], axis=-1)


def class_scores(part_re, part_im, ref_spec, ref_power, inv_noise, inverse):
    middle = ref_spec.shape[-1] // 2
    weighted = ref_spec * inv_noise[None, :, None]
    cross_power = conj_product(
        part_re, part_im, weighted[..., :middle], weighted[..., middle:], "irm,krm->ikm"
    )
    correlation = jnp.einsum("ikm,ma->ika", cross_power, inverse, precision=highest)
    half_norm = 0.5 * jnp.sum(ref_power * inv_noise[None, :], axis=1)
    return correlation - half_norm[None, :, None]


def normaliser(scores):
    local_peak = jnp.max(scores, axis=(1, 2))
    highest_score = lax.pmax(local_peak, "cls")
    total_mass = lax.psum(
        jnp.sum(jnp.exp(scores - highest_score[:, None, None]), axis=(1, 2)), "cls"
    )
    return highest_score + jnp.log(total_mass)


def own_pixels(next_spec, inverse, own_width):
    angles = inverse.shape[1]
    pixel_start = lax.axis_index("dom") * own_width
    spec_row = lax.dynamic_slice_in_dim(next_spec, pixel_start // angles, 1, 1)[:, 0, :]
    columns = lax.dynamic_slice_in_dim(inverse, pixel_start % angles, own_width, 1)
    return jnp.dot(spec_row, columns, precision=highest, preferred_element_type=jnp.float32)


def shards(particles, references, noise_var):
    count_dom = lax.axis_size("dom")
    count_cls = lax.axis_size("cls")
    particle_count, shells, angles = particles.shape
    middle = angles // 2
    forward, inverse, parseval = angle_tables(angles)
    part_spec = jnp.einsum("ira,am->irm", particles, forward, precision=highest)
    part_re = part_spec[..., :middle]
    part_im = part_spec[..., middle:]
    ref_images = lax.all_gather(references, "dom", axis=1, tiled=True)
    local_classes = ref_images.shape[0]
    ref_images = ref_images.reshape(local_classes, shells, angles)
    ref_spec = jnp.einsum("kra,am->krm", ref_images, forward, precision=highest)
    ref_power = jnp.sum(ref_images * ref_images, axis=2)
    inv_noise = 1.0 / noise_var
    scores = class_scores(part_re, part_im, ref_spec, ref_power, inv_noise, inverse)
    log_total = normaliser(scores)
    posterior = jnp.exp(scores - log_total[:, None, None])
    local_counts = jnp.sum(posterior, axis=(0, 2))
    weight_spec = jnp.einsum("ika,am->ikm", posterior, forward, precision=highest)
    sum_spec = conj_product(
        part_re, part_im, weight_spec[..., :middle], weight_spec[..., middle:], "irm,ikm->krm"
    )
    data_shell = jnp.sum(particles * particles, axis=(0, 2)) / count_cls
    count_power = jnp.sum(local_counts[:, None] * ref_power, axis=0)
    cross_shell = jnp.sum(ref_spec * sum_spec * parseval[None, None, :], axis=(0, 2))
    class_term = sum_spec.reshape(local_classes, shells * angles)
    shell_term = data_shell - 2.0 * cross_shell + count_power
    counts = lax.psum(local_counts, "dom")
    shell_total = lax.psum(shell_term, ("dom", "cls"))
    noise_new = shell_total / (particle_count * count_dom * angles)
    owned_sums = lax.psum_scatter(class_term, "dom", scatter_dimension=1, tiled=True)
    owned_spec = owned_sums / (counts[:, None] + 1.0)
    next_spec = lax.all_gather(owned_spec, "dom", axis=1, tiled=True).reshape(
        local_classes, shells, angles
    )
    next_power = jnp.sum(next_spec * next_spec * parseval[None, None, :], axis=2)
    averages = own_pixels(next_spec, inverse, owned_spec.shape[1])
    scores_next = class_scores(part_re, part_im, next_spec, next_power, 1.0 / noise_new, inverse)
    evidence = normaliser(scores_next) - jnp.log(jnp.float32(local_classes * count_cls * angles))
    return (averages, noise_new, evidence)


def solution(mesh):
    placed = (P("dom", None, None), P("cls", "dom"), P())
    return jax.shard_map(
        shards,
        mesh=mesh,
        in_specs=placed,
        out_specs=(P("cls", "dom"), P(), P("dom")),
        check_vma=False,
    )
```

profile of v0, /device:TPU:1, one launch (start us, length us, event | category | flops | bytes accessed | tf_op | source)
XLA Modules:
  0.0 1381.8 jit_solution(2042961747569766877)
XLA Ops:
  8.6 1.7 convolution_bitcast_fusion
  10.9 1.2 multiply_select_fusion
  12.1 196.7 %all-gather.3.cloned.1.call-done = f32[32,16384]{1,0:T(8,128)} async-done(((f32[32,128]{1,0:T(8,128)}), f32[32,16384]{1,0:T(8,128)}) %all-gather.3.cloned.1.call-update) | async-done | bytes 2097168 | tf_op jit(solution)/shard_map/all_gather | solution.py:82
  208.8 2.2 copy.80
  211.4 3.3 bitcast_multiply_fusion.1
  215.4 1.2 fusion.47
  216.6 2.8 copy.46
  219.4 3.1 copy.48
  222.4 5.0 fusion.53
  227.4 3.7 fusion.52
  231.1 4.2 fusion.7
  235.3 4.2 fusion.6
  239.5 1.3 copy.54
  240.7 1.2 copy.55
  241.9 1.4 fusion.50
  243.3 14.9 %pmax.14 = f32[8]{0:T(128)S(1)} all-reduce(f32[8]{0:T(128)S(1)} %get-tuple-element.19), channel_id=1, replica_groups=mesh['dom'=128,'cls'=4] {'cls'}, use_global_device_ids=true, to_apply=%region_3.4 | all-reduce | flops 8 | bytes 64 | tf_op jit(solution)/shard_map/pmax | solution.py:58
  258.4 6.0 psum.28
  266.3 0.8 copy-done.9
  267.1 4.7 fusion.57
  271.8 4.5 fusion.55
  276.3 1.9 copy.56
  278.3 5.9 fusion.56
  284.1 5.0 fusion.54
  289.1 3.7 copy.67
  292.8 2.3 copy.60
  295.1 3.8 copy.66
  298.9 2.3 copy.61
  301.2 2.7 add_bitcast_fusion
  304.0 0.8 copy-done.3
  305.2 2.5 copy.81
  308.6 305.5 %psum.29 = f32[32]{0:T(128)S(1)} all-reduce(f32[32]{0:T(128)S(1)} %fusion.15), channel_id=1, replica_groups=mesh['dom'=128,'cls'=4] {'dom'}, use_global_device_ids=true, to_apply=%region_8.9 | all-reduce | flops 32 | bytes 256 | tf_op jit(solution)/shard_map/psum | solution.py:101
  614.0 305.0 %reduce-scatter.2.cloned.1.call-done = f32[32,128]{1,0:T(8,128)} async-done(((f32[32,16384]{1,0:T(8,128)}), f32[32,128]{1,0:T(8,128)}) %reduce-scatter.2.cloned.1.call-update) | async-done | bytes 16400 | tf_op jit(solution)/shard_map/reduce_scatter | solution.py:104
  919.0 1.4 broadcast_divide_fusion
  920.7 295.9 %all-gather.5.cloned.1.call-done = f32[32,16384]{1,0:T(8,128)} async-done(((f32[32,128]{1,0:T(8,128)}), f32[32,16384]{1,0:T(8,128)}) %all-gather.5.cloned.1.call-update) | async-done | bytes 2097168 | tf_op jit(solution)/shard_map/all_gather | solution.py:106
  1216.7 2.4 copy.82
  1219.5 0.7 multiply_reduce_fusion
  1220.2 110.5 %psum.30 = f32[64]{0:T(128)S(1)} all-reduce(f32[64]{0:T(128)S(1)} %subtract_add_fusion), channel_id=1, replica_groups=mesh['dom'=128,'cls'=4] {'dom','cls'}, use_global_device_ids=true, to_apply=%region_12.13 | all-reduce | flops 64 | bytes 512 | tf_op jit(solution)/shard_map/psum | solution.py:102
  1331.7 1.6 fusion.46
  1333.3 4.0 copy.69
  1337.3 5.8 fusion.59
  1343.1 4.1 copy.71
  1347.1 5.1 fusion.58
  1352.3 4.2 fusion.4
  1356.5 3.4 fusion.3
  1359.8 1.2 copy.77
  1361.7 5.8 pmax.15
  1367.8 5.8 psum.31
  1374.1 0.8 fusion.27
  (87 shorter events, 9.5 us)
Async XLA Ops:
  7.2 201.7 %all-gather.3.cloned.1.call-start = ((), (), s32[]{:S(2)}) async-start(), calls=%async_computation.1 | async-start | bytes 2113536 | tf_op jit(solution)/shard_map/all_gather | solution.py:82
  7.9 911.1 %reduce-scatter.2.cloned.1.call-start = ((), (), s32[]{:S(2)}) async-start(), calls=%async_computation.2 | async-start | bytes 2113536 | tf_op jit(solution)/shard_map/reduce_scatter | solution.py:104
  8.0 227.3 %copy-start.18 = (pred[128]{0:T(512)(128)(4,1)}, pred[128]{0:T(512)(128)(4,1)S(1)}, u32[]{:S(2)}) copy-start(pred[128]{0:T(512)(128)(4,1)S(1)} %iota_compare_fusion) | copy-start | bytes 388
  8.0 2.9 copy-start.24
  8.5 202.9 %copy-start.14 = (f32[256,128]{1,0:T(8,128)}, f32[256,128]{1,0:T(8,128)S(1)}, u32[]{:S(2)}) copy-start(f32[256,128]{1,0:T(8,128)S(1)} %get-tuple-element.23) | copy-start | bytes 393220
  8.5 202.9 %copy-start.16 = (f32[256,128]{1,0:T(8,128)}, f32[256,128]{1,0:T(8,128)S(1)}, u32[]{:S(2)}) copy-start(f32[256,128]{1,0:T(8,128)S(1)} %get-tuple-element.24) | copy-start | bytes 393220
  10.8 200.2 %copy-start.22 = (f32[128]{0:T(128)}, f32[128]{0:T(128)S(1)}, u32[]{:S(2)}) copy-start(f32[128]{0:T(128)S(1)} %select_multiply_fusion) | copy-start | bytes 1540
  227.4 3.7 copy-start.2
  239.4 25.5 %copy-start.15 = (f32[256,128]{1,0:T(8,128)S(1)}, f32[256,128]{1,0:T(8,128)}, u32[]{:S(2)}) copy-start(f32[256,128]{1,0:T(8,128)} %copy-done.14) | copy-start | bytes 393220
  239.4 25.5 %copy-start.17 = (f32[256,128]{1,0:T(8,128)S(1)}, f32[256,128]{1,0:T(8,128)}, u32[]{:S(2)}) copy-start(f32[256,128]{1,0:T(8,128)} %copy-done.16) | copy-start | bytes 393220
  264.4 0.5 copy-start.20
  266.3 0.8 copy-start.9
  278.2 5.9 copy-start.10
  295.1 3.8 copy-start.7
  303.8 1.0 copy-start.3
  303.9 1.3 copy-start.5
  307.7 0.7 copy-start.21
  307.7 612.7 %copy-start.23 = (f32[128]{0:T(128)S(1)}, f32[128]{0:T(128)}, u32[]{:S(2)}) copy-start(f32[128]{0:T(128)} %copy-done.22) | copy-start | bytes 1540
  307.7 612.8 %copy-start.11 = (f32[8,64,256]{2,1,0:T(8,128)S(1)}, f32[8,64,256]{2,1,0:T(8,128)}, u32[]{:S(2)}) copy-start(f32[8,64,256]{2,1,0:T(8,128)} %param.3) | copy-start | bytes 1572868
  307.7 908.9 %all-gather.5.cloned.1.call-start = ((), (), s32[]{:S(2)}) async-start(), calls=%async_computation.3 | async-start | bytes 2113536 | tf_op jit(solution)/shard_map/all_gather | solution.py:106
  1216.7 2.4 copy-start.4
  1216.7 2.4 copy-start.6
  1216.7 2.9 copy-start.8
  1347.1 5.1 copy-start.1
  1347.1 5.1 copy-start.19
  1352.3 4.2 copy-start
  1352.3 4.2 copy-start.12
  1356.4 4.8 copy-start.13
Sparse Core Ops, SparseCore 0:
  12.3 196.4 all-gather.2
  307.9 611.0 reduce-scatter.1
  924.7 291.9 all-gather.4
where the time goes:
time: 1390 us; the launch traced here: 1380 us
  waiting for transfers between devices  798 us (57%)
  blocking collectives  448 us (32%)
  matrix products  63.6 us (5%)
  local copies, waits for them, and re-layouts  46.8 us (3%)
  between operations  14.5 us (1%)
    psum x1, blocking collectives, shards(): counts = lax.psum(local_counts, 'dom')  305 us
    reduce_scatter x1, waiting for transfers between devices, shards(): lax.psum_scatter(class_term, 'dom', scatter_dimension=1, tiled=True)  305 us
    all_gather x1, waiting for transfers between devices, shards(): lax.all_gather(owned_spec, 'dom', axis=1, tiled=True)  296 us
    all_gather x1, waiting for transfers between devices, shards(): ref_images = lax.all_gather(references, 'dom', axis=1, tiled=True)  197 us
    psum x1, blocking collectives, shards(): shell_total = lax.psum(shell_term, ('dom', 'cls'))  111 us
  transfers between devices with their start and end apart: 3, of which 3 were waited for; matrix products, arithmetic and copies ran while one was open for 0% of the time, Pallas kernels for 0%

commit v1 on v0

v1 whole, which is shorter than its diff:
```python
import jax
import jax.numpy as jnp
import numpy as np
from jax import lax
from jax.experimental import pallas as pl
from jax.experimental.pallas import tpu as pltpu
from jax.sharding import Mesh, PartitionSpec as P

GROUP = ("near", "hx", "cls")
FAR = 8
NEAR = 64
SHELLS = 64
ANGLES = 256
HALF = ANGLES // 2
CLASSES = 128
OWN_CLASSES = 32
OWN_PARTICLES = 2
PARTICLES = 1024
LANES = 128


def dot(left, right, contract=((1,), (0,))):
    return lax.dot_general(
        left,
        right,
        (contract, ((), ())),
        precision=lax.Precision.HIGHEST,
        preferred_element_type=jnp.float32,
    )


def angle_tables():
    angle = np.arange(ANGLES)
    slot = np.arange(HALF)
    radians = (slot[:, None] * angle[None, :] % ANGLES) * (2.0 * np.pi / ANGLES)
    sine = -np.sin(radians)
    sine[0] = np.where(angle % 2 == 0, 1.0, -1.0)
    forward = np.concatenate([np.cos(radians), sine], axis=0)
    weight = np.where(slot == 0, 1.0, 2.0) / ANGLES
    inverse = forward * np.concatenate([weight, weight])[:, None]
    return (
        jnp.asarray(forward.astype(np.float32)),
        jnp.asarray(np.ascontiguousarray(inverse.T).astype(np.float32)),
    )


def rows(base, count, stride):
    return pl.ds(base, count, stride=stride)


def halves(image, part):
    return image[:, part * SHELLS : (part + 1) * SHELLS]


SPREAD = 6
MODEL = 33
CROSS = 8
WEIGHT = 9
SUMS = 34
FINAL = 10


def spread_kernel(place, inv_noise, forward, particles, references, out):
    quarter, half, shell = place[0], place[1], place[2]
    images = particles[pl.ds(quarter * OWN_PARTICLES, OWN_PARTICLES)]
    images = images.reshape(OWN_PARTICLES * SHELLS, ANGLES)
    spectrum = dot(forward[...], images, ((1,), (1,)))
    for i in range(OWN_PARTICLES):
        both = jnp.concatenate(
            [halves(spectrum[:HALF], i), halves(spectrum[HALF:], i)], axis=1
        )
        for m in range(2):
            out[rows(i * 2 + m, NEAR, SPREAD), :] = both[m * NEAR : (m + 1) * NEAR]
    own = references[...]
    table = forward[:, pl.ds(pl.multiple_of(half * HALF, HALF), HALF)]
    model = dot(table, own, ((1,), (1,)))
    pieces = []
    for m in range(2):
        for part in range(2):
            start = part * HALF + m * NEAR
            pieces.append(model[start : start + NEAR])
    out[rows(4, NEAR, SPREAD), :] = jnp.concatenate(pieces, axis=1)
    power = dot(jnp.full((8, LANES), 0.5, jnp.float32), own * own, ((1,), (1,)))
    power = jnp.concatenate([power] * 4, axis=1) * inv_noise[shell]
    lane = lax.broadcasted_iota(jnp.int32, power.shape, 1)
    power = jnp.where(lane // OWN_CLASSES == quarter, power, 0.0)
    out[rows(5, NEAR, SPREAD), :] = jnp.broadcast_to(power[:1], (NEAR, LANES))


def model_kernel(spread, out):
    by_class = []
    for c in range(4):
        first = spread[rows(c * SPREAD + 4, 8, 8 * SPREAD), :]
        second = spread[rows((c + 4) * SPREAD + 4, 8, 8 * SPREAD), :]
        by_class.append(first + second)
    power = jnp.sum(spread[rows(5, NEAR, SPREAD), :], axis=0, keepdims=True)
    pieces = []
    for j in range(4):
        span = slice(j * OWN_CLASSES, (j + 1) * OWN_CLASSES)
        pieces.append(jnp.concatenate([part[:, span] for part in by_class], axis=1))
    block = jnp.concatenate(pieces, axis=0)
    for far in range(FAR):
        out[far * MODEL : far * MODEL + 32, :] = block
        out[far * MODEL + 32 : far * MODEL + 33, :] = power


def model_rows(model, stride, j):
    return jnp.concatenate(
        [model[far * stride + j * 8 : far * stride + j * 8 + 8, :] for far in range(FAR)],
        axis=0,
    )


def particle_rows(spread, m):
    return jnp.concatenate(
        [spread[rows(i * 2 + m, NEAR, SPREAD), :] for i in range(OWN_PARTICLES)], axis=0
    )


def cross_rows(left, real, imag, packed):
    top = jnp.concatenate([real, jnp.where(packed, 0.0, -imag)], axis=1)
    bottom = jnp.concatenate(
        [jnp.where(packed, 0.0, imag), jnp.where(packed, imag, real)], axis=1
    )
    return dot(left, jnp.concatenate([top, bottom], axis=0))


def store_cross(out, stride, m, cross):
    for i in range(OWN_PARTICLES):
        for part in range(2):
            value = cross[i * NEAR : (i + 1) * NEAR, part * LANES : (part + 1) * LANES]
            out[rows(i * 4 + m * 2 + part, NEAR, stride), :] = value


def cross_kernel(place, inv_noise, spread, model, out, half_norm):
    leading = place[3] == 0
    scale = inv_noise[...]
    for m in range(2):
        real = model_rows(model, MODEL, 2 * m) * scale
        imag = model_rows(model, MODEL, 2 * m + 1) * scale
        packed = jnp.logical_and(leading, m == 0)
        store_cross(out, CROSS, m, cross_rows(particle_rows(spread, m), real, imag, packed))
    power = jnp.sum(model[rows(32, FAR, MODEL), :], axis=0, keepdims=True)
    half_norm[...] = jnp.broadcast_to(power, (8, LANES))


def group_scores(cross, stride, inverse, half_norm):
    columns = []
    for i in range(OWN_PARTICLES):
        parts = [
            cross[rows(i * 4 + m * 2 + part, NEAR, stride), :]
            for part in range(2)
            for m in range(2)
        ]
        columns.append(jnp.concatenate(parts, axis=0))
    scores = dot(inverse[...], jnp.concatenate(columns, axis=1))
    return [scores[:, i * LANES : (i + 1) * LANES] - half_norm for i in range(OWN_PARTICLES)]


def whole(reduce, value):
    return reduce(reduce(value, axis=0, keepdims=True), axis=1, keepdims=True)


def posterior_kernel(cross, half_norm, forward, inverse, out):
    posterior = []
    counts = jnp.zeros((1, LANES), jnp.float32)
    for scores in group_scores(cross, CROSS, inverse, half_norm[:1]):
        mass = jnp.exp(scores - whole(jnp.max, scores))
        mass = mass / whole(jnp.sum, mass)
        counts = counts + jnp.sum(mass, axis=0, keepdims=True)
        posterior.append(mass)
    spectrum = dot(forward[...], jnp.concatenate(posterior, axis=1))
    for i in range(OWN_PARTICLES):
        for m in range(2):
            for part in range(2):
                start = part * HALF + m * NEAR
                out[rows(i * 4 + m * 2 + part, NEAR, WEIGHT), :] = spectrum[
                    start : start + NEAR, i * LANES : (i + 1) * LANES
                ]
    out[rows(8, NEAR, WEIGHT), :] = jnp.broadcast_to(counts, (NEAR, LANES))


def sums_kernel(place, spread, model, weight, out):
    leading = place[3] == 0
    counts = jnp.sum(weight[rows(8, NEAR, WEIGHT), :], axis=0, keepdims=True)
    residual = jnp.zeros((SHELLS, LANES), jnp.float32)
    for m in range(2):
        packed = jnp.logical_and(leading, m == 0)
        share = jnp.where(packed, 1.0, 2.0) / ANGLES
        left = particle_rows(spread, m)
        sides = []
        for part in range(2):
            sides.append(
                jnp.concatenate(
                    [
                        weight[rows(i * 4 + m * 2 + part, NEAR, WEIGHT), :]
                        for i in range(OWN_PARTICLES)
                    ],
                    axis=0,
                )
            )
        left_t = left.T
        product = dot(left_t, jnp.concatenate(sides, axis=1))
        real_real = product[:SHELLS, :LANES]
        imag_real = product[SHELLS:, :LANES]
        real_imag = product[:SHELLS, LANES:]
        imag_imag = product[SHELLS:, LANES:]
        real = real_real + jnp.where(packed, 0.0, imag_imag)
        imag = jnp.where(packed, imag_imag, imag_real - real_imag)
        energy = jnp.sum(left_t * left_t, axis=1, keepdims=True)
        residual = residual + (energy[:SHELLS] + energy[SHELLS:]) * (share / LANES)
        for part, value in ((0, real), (1, imag)):
            j = 2 * m + part
            ref = model_rows(model, MODEL, j)
            residual = residual + share * ref * (counts * ref - 2.0 * value)
            for far in range(FAR):
                start = far * SUMS + j * 8
                out[start : start + 8, :] = value[far * 8 : far * 8 + 8]
    power = dot(jnp.ones((8, LANES), jnp.float32), residual, ((1,), (1,)))
    power = jnp.concatenate([power, jnp.zeros_like(power)], axis=1)
    for far in range(FAR):
        start = far * SUMS + 32
        out[start : start + 1, :] = counts
        out[start + 1 : start + 2, :] = power[:1]


def average_kernel(sums, averages, spread_averages, residual):
    total = sums[0:SUMS, :]
    for far in range(1, FAR):
        total = total + sums[far * SUMS : (far + 1) * SUMS, :]
    block = total[:32] / (total[32:33] + 1.0)
    averages[...] = block
    for far in range(FAR):
        spread_averages[far * 32 : far * 32 + 32, :] = block
    residual[...] = jnp.broadcast_to(total[33:34], (NEAR, LANES))


def next_kernel(place, spread, averages, model, residual, out, noise_out):
    leading = place[3] == 0
    noise = jnp.sum(residual[...], axis=0, keepdims=True)[:, :SHELLS]
    noise = noise / (PARTICLES * ANGLES)
    noise_out[...] = noise
    row = lax.broadcasted_iota(jnp.int32, (SHELLS, SHELLS), 0)
    column = lax.broadcasted_iota(jnp.int32, (SHELLS, SHELLS), 1)
    scale = 1.0 / jnp.sum(jnp.where(row == column, noise, 0.0), axis=1, keepdims=True)
    half_norm = jnp.zeros((SHELLS, LANES), jnp.float32)
    for m in range(2):
        packed = jnp.logical_and(leading, m == 0)
        share = jnp.where(packed, 0.5, 1.0) / ANGLES
        real = model_rows(model, 32, 2 * m)
        imag = model_rows(model, 32, 2 * m + 1)
        half_norm = half_norm + share * scale * (real * real + imag * imag)
        cross = cross_rows(particle_rows(spread, m), real * scale, imag * scale, packed)
        store_cross(out, FINAL, m, cross)
    half_norm = jnp.sum(half_norm, axis=0, keepdims=True)
    out[rows(8, NEAR, FINAL), :] = jnp.broadcast_to(half_norm, (NEAR, LANES))
    own = [averages[j * 8 : j * 8 + 8, :] for j in range(4)]
    for c in range(4):
        span = slice(c * OWN_CLASSES, (c + 1) * OWN_CLASSES)
        piece = jnp.concatenate([part[:, span] for part in own], axis=1)
        for side in range(2):
            out[rows((side * 4 + c) * FINAL + 9, 8, 8 * FINAL), :] = piece


def evidence_kernel(place, final, inverse, averages, evidence):
    quarter, half = place[0], place[1]
    half_norm = jnp.sum(final[rows(8, NEAR, FINAL), :], axis=0, keepdims=True)
    lane = lax.broadcasted_iota(jnp.int32, (1, LANES), 1)
    found = jnp.zeros((1, LANES), jnp.float32)
    for i, scores in enumerate(group_scores(final, FINAL, inverse, half_norm)):
        peak = whole(jnp.max, scores)
        total = peak + jnp.log(whole(jnp.sum, jnp.exp(scores - peak)))
        total = total - jnp.log(jnp.full((1, 1), CLASSES * ANGLES, jnp.float32))
        found = found + jnp.where(lane == quarter * OWN_PARTICLES + i, total, 0.0)
    evidence[...] = found
    packed = final[rows(9, NEAR, FINAL), :]
    pieces = []
    for part in range(2):
        for m in range(2):
            j = 2 * m + part
            pieces.append(packed[:, j * OWN_CLASSES : (j + 1) * OWN_CLASSES])
    spectrum = jnp.concatenate(pieces, axis=0)
    table = inverse[pl.ds(pl.multiple_of(half * HALF, HALF), HALF), :]
    averages[...] = dot(table, spectrum).T


SMEM = pl.BlockSpec(memory_space=pltpu.SMEM)
VMEM = pl.BlockSpec(memory_space=pltpu.VMEM)


def call(kernel, shapes, *operands, scalars=0):
    outs = [jax.ShapeDtypeStruct(shape, jnp.float32) for shape in shapes]
    result = pl.pallas_call(
        kernel,
        out_shape=outs if len(outs) > 1 else outs[0],
        in_specs=[SMEM] * scalars + [VMEM] * (len(operands) - scalars),
        out_specs=[VMEM] * len(outs) if len(outs) > 1 else VMEM,
        compiler_params=pltpu.CompilerParams(vmem_limit_bytes=32 * 1024 * 1024),
    )(*operands)
    return result


def exchange(value, axes, count):
    sent = value.reshape(count, 1, value.size // count)
    got = lax.all_to_all(sent, axes, 0, 0, tiled=True)
    return got.reshape(value.shape)


def shards(particles, references, noise_var):
    forward, inverse = angle_tables()
    near, hx, cls = (lax.axis_index(name) for name in GROUP)
    far = lax.axis_index("far")
    shell = far * 8 + near * 4 + hx // 2
    leader = near * 32 + hx * 4 + cls
    place = jnp.stack([cls, hx % 2, shell, leader]).astype(jnp.int32)
    inv_noise = 1.0 / noise_var
    with jax.named_scope("spread"):
        spread = call(
            spread_kernel,
            [(NEAR * SPREAD, LANES)],
            place,
            inv_noise,
            forward,
            particles,
            references,
            scalars=2,
        )
        spread = exchange(spread, GROUP, NEAR)
    with jax.named_scope("model"):
        model = call(model_kernel, [(FAR * MODEL, LANES)], spread)
        model = exchange(model, "far", FAR)
    with jax.named_scope("cross"):
        cross, half_norm = call(
            cross_kernel,
            [(NEAR * CROSS, LANES), (8, LANES)],
            place,
            inv_noise.reshape(SHELLS, 1),
            spread,
            model,
            scalars=1,
        )
        cross = exchange(cross, GROUP, NEAR)
    with jax.named_scope("posterior"):
        weight = call(
            posterior_kernel, [(NEAR * WEIGHT, LANES)], cross, half_norm, forward, inverse
        )
        weight = exchange(weight, GROUP, NEAR)
    with jax.named_scope("sums"):
        sums = call(
            sums_kernel, [(FAR * SUMS, LANES)], place, spread, model, weight, scalars=1
        )
        sums = exchange(sums, "far", FAR)
    with jax.named_scope("averages"):
        own, next_model, residual = call(
            average_kernel, [(32, LANES), (FAR * 32, LANES), (NEAR, LANES)], sums
        )
        residual = exchange(residual, GROUP, NEAR)
        next_model = exchange(next_model, "far", FAR)
    with jax.named_scope("next"):
        final, noise_new = call(
            next_kernel,
            [(NEAR * FINAL, LANES), (1, SHELLS)],
            place,
            spread,
            own,
            next_model,
            residual,
            scalars=1,
        )
        final = exchange(final, GROUP, NEAR)
    with jax.named_scope("evidence"):
        averages, evidence = call(
            evidence_kernel,
            [(OWN_CLASSES, LANES), (1, LANES)],
            place,
            final,
            inverse,
            scalars=1,
        )
        evidence = lax.psum(evidence[0, :8], "cls")
    return averages, noise_new.reshape(SHELLS), evidence


def solution(mesh):
    split = Mesh(mesh.devices.reshape(FAR, 2, 8, 4), ("far", "near", "hx", "cls"))
    dom = ("far", "near", "hx")
    return jax.shard_map(
        shards,
        mesh=split,
        in_specs=(P(dom, None, None), P("cls", dom), P()),
        out_specs=(P("cls", dom), P(), P(dom)),
        check_vma=False,
    )
```

time: 1390 us -> 162 us (0.12)
  waiting for transfers between devices: 798 us -> 13 us
  blocking collectives: 448 us -> 123 us
  matrix products: 63.6 us -> 0 us
  local copies, waits for them, and re-layouts: 46.8 us -> 2.75 us
    all_gather x2 -> x0, waiting for transfers between devices: 493 us -> none  [the longest x1 296 us: shards(): lax.all_gather(owned_spec, 'dom', axis=1, tiled=True)]
    psum x4 -> x1, blocking collectives: 428 us -> 6.23 us  [shards(): evidence = lax.psum(evidence[0, :8], 'cls')]
    reduce_scatter x1 -> x0, waiting for transfers between devices: 305 us -> none  [shards(): lax.psum_scatter(class_term, 'dom', scatter_dimension=1, tiled=True)]
    all_to_all x0 -> x7, blocking collectives: none -> 116 us  [exchange(): got = lax.all_to_all(sent, axes, 0, 0, tiled=True)]
    dot_general x18 -> x0, matrix products: 63.6 us -> none  [the longest x3 16.6 us: conj_product(): imag_real = jnp.einsum(pattern, left_im, right_re, precision=highest)]
    pmax x2 -> x0, blocking collectives: 20.7 us -> none  [normaliser(): highest_score = lax.pmax(local_peak, 'cls')]
    slice x12 -> x0, local copies, waits for them, and re-layouts: 20.1 us -> none  [the longest x4 9.61 us: class_scores(): weighted[..., :middle]]
  transfers between devices with their start and end apart: 3 -> 1, of which waited for: 3 -> 1; matrix products, arithmetic and copies ran while one was open for 0% -> 0% of each run, Pallas kernels for 0% -> 0%
where the time goes in v1:
time: 162 us
  blocking collectives  123 us (76%)
  starting transfers between devices  13.8 us (9%)
  waiting for transfers between devices  13 us (8%)
  Pallas kernels  8.57 us (5%)
  local copies, waits for them, and re-layouts  2.75 us (2%)
    all_to_all x7, blocking collectives, exchange(): got = lax.all_to_all(sent, axes, 0, 0, tiled=True)  116 us
    all_to_all x1, starting transfers between devices, exchange(): got = lax.all_to_all(sent, axes, 0, 0, tiled=True)  13.8 us
    all_to_all x1, waiting for transfers between devices, exchange(): got = lax.all_to_all(sent, axes, 0, 0, tiled=True)  13 us
    pallas_call x8, Pallas kernels, call(): pl.pallas_call(kernel, out_shape=outs if len(outs) > 1 else outs[0], in_s...  8.57 us
    psum x1, blocking collectives, shards(): evidence = lax.psum(evidence[0, :8], 'cls')  6.23 us
  transfers between devices with their start and end apart: 1, of which 1 were waited for; matrix products, arithmetic and copies ran while one was open for 0% of the time, Pallas kernels for 0%

profile of v1, /device:TPU:1, one launch (start us, length us, event | category | flops | bytes accessed | tf_op | source)
XLA Modules:
  0.0 161.5 jit_solution(9868451847939041395)
XLA Ops:
  0.7 0.0 copy-start.5
  0.7 0.0 copy-start.4
  0.7 0.6 copy-done.5
  1.3 0.1 pad_add_fusion.place
  1.4 0.0 copy-done.4
  1.4 0.0 copy-start
  1.4 1.0 copy-done
  2.3 0.0 copy-start.3
  2.4 1.0 copy-done.3
  3.4 1.1 spread.1
  4.5 19.3 %all_to_all.40 = f32[64,1,768]{2,1,0:T(1,128)S(1)} all-to-all(f32[64,1,768]{2,1,0:T(1,128)S(1)} %bitcast.37), channel_id=1, replica_groups=mesh['far'=8,'near'=2,'hx'=8,'cls'=4] {'near','hx','cls'}, dimensions={0} | all-to-all | bytes 393216 | tf_op jit(solution)/shard_map/spread/all_to_all | solution.py:305
  23.9 0.7 model.1
  24.6 13.8 %all-to-all-start.1 = ((f32[8,1,4224]{2,1,0:T(1,128)}), f32[8,1,4224]{2,1,0:T(1,128)S(1)}, u32[]{:S(2)}, u32[]{:S(2)}) async-start(f32[8,1,4224]{2,1,0:T(1,128)} %bitcast.6), calls=%async_computation.1 | async-start | bytes 270336 | tf_op jit(solution)/shard_map/model/all_to_all | solution.py:305
  38.5 0.1 copy.11.inv_noise
  38.5 13.0 %all-to-all-done.1 = f32[8,1,4224]{2,1,0:T(1,128)S(1)} async-done(((f32[8,1,4224]{2,1,0:T(1,128)}), f32[8,1,4224]{2,1,0:T(1,128)S(1)}, u32[]{:S(2)}, u32[]{:S(2)}) %all-to-all-start.1) | async-done | bytes 135200 | tf_op jit(solution)/shard_map/model/all_to_all | solution.py:305
  51.6 1.0 cross.1
  52.6 0.0 copy-start.1
  52.6 0.0 copy-start.2
  52.6 17.9 %all_to_all.41 = f32[64,1,1024]{2,1,0:T(1,128)S(1)} all-to-all(f32[64,1,1024]{2,1,0:T(1,128)S(1)} %bitcast.42), channel_id=1, replica_groups=mesh['far'=8,'near'=2,'hx'=8,'cls'=4] {'near','hx','cls'}, dimensions={0} | all-to-all | bytes 524288 | tf_op jit(solution)/shard_map/cross/all_to_all | solution.py:305
  70.5 0.0 copy-done.1
  70.5 0.0 copy-done.2
  70.5 1.4 posterior.1
  71.9 14.3 %all_to_all.42 = f32[64,1,1152]{2,1,0:T(1,128)S(1)} all-to-all(f32[64,1,1152]{2,1,0:T(1,128)S(1)} %bitcast.34), channel_id=1, replica_groups=mesh['far'=8,'near'=2,'hx'=8,'cls'=4] {'near','hx','cls'}, dimensions={0} | all-to-all | bytes 589824 | tf_op jit(solution)/shard_map/posterior/all_to_all | solution.py:305
  86.2 1.1 sums.1
  87.3 15.5 %all_to_all.43 = f32[8,1,4352]{2,1,0:T(1,128)S(1)} all-to-all(f32[8,1,4352]{2,1,0:T(1,128)S(1)} %bitcast.39), channel_id=1, replica_groups=mesh['far'=8,'near'=2,'hx'=8,'cls'=4] {'far'}, dimensions={0} | all-to-all | bytes 278528 | tf_op jit(solution)/shard_map/sums/all_to_all | solution.py:305
  102.8 15.9 %all_to_all.44 = f32[64,1,128]{2,1,0:T(1,128)S(1)} all-to-all(f32[64,1,128]{2,1,0:T(1,128)S(1)} %bitcast.45), channel_id=1, replica_groups=mesh['far'=8,'near'=2,'hx'=8,'cls'=4] {'near','hx','cls'}, dimensions={0} | all-to-all | bytes 65536 | tf_op jit(solution)/shard_map/averages/all_to_all | solution.py:305
  118.7 15.7 %all_to_all.45 = f32[8,1,4096]{2,1,0:T(1,128)S(1)} all-to-all(f32[8,1,4096]{2,1,0:T(1,128)S(1)} %bitcast.44), channel_id=1, replica_groups=mesh['far'=8,'near'=2,'hx'=8,'cls'=4] {'far'}, dimensions={0} | all-to-all | bytes 262144 | tf_op jit(solution)/shard_map/averages/all_to_all | solution.py:305
  134.4 1.4 next.1
  135.8 17.7 %all_to_all.46 = f32[64,1,1280]{2,1,0:T(1,128)S(1)} all-to-all(f32[64,1,1280]{2,1,0:T(1,128)S(1)} %bitcast.41), channel_id=1, replica_groups=mesh['far'=8,'near'=2,'hx'=8,'cls'=4] {'near','hx','cls'}, dimensions={0} | all-to-all | bytes 655360 | tf_op jit(solution)/shard_map/next/all_to_all | solution.py:305
  153.5 1.8 %evidence.1 = (f32[32,128]{1,0:T(8,128)}, f32[1,128]{1,0:T(1,128)S(1)}) custom-call(s32[4]{0:T(128)S(1)} %pad_add_fusion.place, f32[640,128]{1,0:T(8,128)S(1)} %bitcast.31, f32[256,256]{1,0:T(8,128)S(1)} %copy-done.2), custom_call_target="tpu_custom_call" | custom-call | tf_op jit(solution)/shard_map/evidence/pallas_call | solution.py:293
  155.3 6.2 %psum.7 = f32[8]{0:T(128)} all-reduce(f32[8]{0:T(128)S(1)} %slice_bitcast_fusion), channel_id=1, replica_groups=mesh['far'=8,'near'=2,'hx'=8,'cls'=4] {'cls'}, use_global_device_ids=true, to_apply=%region_0.1 | all-reduce | flops 8 | bytes 64 | tf_op jit(solution)/shard_map/evidence/psum | solution.py:380
  (4 shorter events, 0.0 us)
Async XLA Ops:
  0.7 0.7 copy-start.5
  0.7 0.7 copy-start.4
  1.4 1.0 copy-start
  2.3 1.0 copy-start.3
  24.6 26.9 %all-to-all-start.1 = ((f32[8,1,4224]{2,1,0:T(1,128)}), f32[8,1,4224]{2,1,0:T(1,128)S(1)}, u32[]{:S(2)}, u32[]{:S(2)}) async-start(f32[8,1,4224]{2,1,0:T(1,128)} %bitcast.6), calls=%async_computation.1 | async-start | bytes 270336 | tf_op jit(solution)/shard_map/model/all_to_all | solution.py:305
  52.6 17.9 %copy-start.1 = (f32[256,256]{1,0:T(8,128)S(1)}, f32[256,256]{1,0:T(8,128)}, u32[]{:S(2)}) copy-start(f32[256,256]{1,0:T(8,128)} %constant.55.clone.forward) | copy-start | bytes 786436
  52.6 17.9 %copy-start.2 = (f32[256,256]{1,0:T(8,128)S(1)}, f32[256,256]{1,0:T(8,128)}, u32[]{:S(2)}) copy-start(f32[256,256]{1,0:T(8,128)} %constant.56.clone.inverse) | copy-start | bytes 786436

commit v2 on v1

--- a/solution.py
+++ b/solution.py
@@ -6,7 +6,7 @@
 from jax.experimental.pallas import tpu as pltpu
 from jax.sharding import Mesh, PartitionSpec as P
 
-GROUP = ("near", "hx", "cls")
+GROUP = ("near", "h", "x", "cls")
 FAR = 8
 NEAR = 64
 SHELLS = 64
@@ -44,6 +44,12 @@
     )
 
 
+def place():
+    near, h, x, cls = (lax.axis_index(name) for name in GROUP)
+    shell = lax.axis_index("far") * 8 + near * 4 + h * 2 + lax.shift_right_logical(x, 1)
+    return cls, lax.bitwise_and(x, 1), shell, near * 32 + h * 16 + x * 4 + cls
+
+
 def rows(base, count, stride):
     return pl.ds(base, count, stride=stride)
 
@@ -56,22 +62,49 @@
 MODEL = 33
 CROSS = 8
 WEIGHT = 9
-SUMS = 34
+SUMS = 33
+NEXT = 33
 FINAL = 10
 
 
-def spread_kernel(place, inv_noise, forward, particles, references, out):
-    quarter, half, shell = place[0], place[1], place[2]
-    images = particles[pl.ds(quarter * OWN_PARTICLES, OWN_PARTICLES)]
-    images = images.reshape(OWN_PARTICLES * SHELLS, ANGLES)
-    spectrum = dot(forward[...], images, ((1,), (1,)))
+def inverse_column(noise):
+    row = lax.broadcasted_iota(jnp.int32, (SHELLS, SHELLS), 0)
+    column = lax.broadcasted_iota(jnp.int32, (SHELLS, SHELLS), 1)
+    return 1.0 / jnp.sum(jnp.where(row == column, noise, 0.0), axis=1, keepdims=True)
+
+
+def spread_kernel(
+    noise_ref, table_ref, particles, references, out, noise, forward, images, own_ref, sems
+):
+    quarter, half, shell, _ = place()
+    first = quarter * OWN_PARTICLES
+    copies = [
+        pltpu.make_async_copy(noise_ref, noise, sems.at[0]),
+        pltpu.make_async_copy(references, own_ref, sems.at[1]),
+    ]
+    for i in range(OWN_PARTICLES):
+        copies.append(
+            pltpu.make_async_copy(particles.at[first + i], images.at[i], sems.at[2 + i])
+        )
+    for i in range(4):
+        span = pl.ds(i * NEAR, NEAR)
+        copies.append(
+            pltpu.make_async_copy(table_ref.at[span], forward.at[span], sems.at[4 + i])
+        )
+    for copy in copies:
+        copy.start()
+    for copy in copies:
+        copy.wait()
+    spectrum = dot(
+        forward[...], images[...].reshape(OWN_PARTICLES * SHELLS, ANGLES), ((1,), (1,))
+    )
     for i in range(OWN_PARTICLES):
         both = jnp.concatenate(
             [halves(spectrum[:HALF], i), halves(spectrum[HALF:], i)], axis=1
         )
         for m in range(2):
             out[rows(i * 2 + m, NEAR, SPREAD), :] = both[m * NEAR : (m + 1) * NEAR]
-    own = references[...]
+    own = own_ref[...]
     table = forward[:, pl.ds(pl.multiple_of(half * HALF, HALF), HALF)]
     model = dot(table, own, ((1,), (1,)))
     pieces = []
@@ -81,10 +114,14 @@
             pieces.append(model[start : start + NEAR])
     out[rows(4, NEAR, SPREAD), :] = jnp.concatenate(pieces, axis=1)
     power = dot(jnp.full((8, LANES), 0.5, jnp.float32), own * own, ((1,), (1,)))
-    power = jnp.concatenate([power] * 4, axis=1) * inv_noise[shell]
+    lane = lax.broadcasted_iota(jnp.int32, (1, SHELLS), 1)
+    own_noise = jnp.sum(jnp.where(lane == shell, noise[...], 0.0), axis=1, keepdims=True)
+    power = jnp.concatenate([power] * 4, axis=1) * (1.0 / own_noise)
     lane = lax.broadcasted_iota(jnp.int32, power.shape, 1)
     power = jnp.where(lane // OWN_CLASSES == quarter, power, 0.0)
-    out[rows(5, NEAR, SPREAD), :] = jnp.broadcast_to(power[:1], (NEAR, LANES))
+    passed = jnp.concatenate([noise[...], jnp.zeros((1, SHELLS), jnp.float32)], axis=1)
+    power = power[:1] + jnp.where(quarter == 3, passed, 0.0)
+    out[rows(5, NEAR, SPREAD), :] = jnp.broadcast_to(power, (NEAR, LANES))
 
 
 def model_kernel(spread, out):
@@ -93,7 +130,11 @@
         first = spread[rows(c * SPREAD + 4, 8, 8 * SPREAD), :]
         second = spread[rows((c + 4) * SPREAD + 4, 8, 8 * SPREAD), :]
         by_class.append(first + second)
-    power = jnp.sum(spread[rows(5, NEAR, SPREAD), :], axis=0, keepdims=True)
+    power = spread[rows(5, NEAR, SPREAD), :]
+    lane = lax.broadcasted_iota(jnp.int32, power.shape, 1)
+    sender = lax.broadcasted_iota(jnp.int32, power.shape, 0)
+    own = lax.shift_right_logical(lane, 5) == lax.bitwise_and(sender, 3)
+    power = jnp.sum(jnp.where(own, power, 0.0), axis=0, keepdims=True)
     pieces = []
     for j in range(4):
         span = slice(j * OWN_CLASSES, (j + 1) * OWN_CLASSES)
@@ -132,9 +173,10 @@
             out[rows(i * 4 + m * 2 + part, NEAR, stride), :] = value
 
 
-def cross_kernel(place, inv_noise, spread, model, out, half_norm):
-    leading = place[3] == 0
-    scale = inv_noise[...]
+def cross_kernel(spread, model, out, half_norm):
+    leading = place()[3] == 0
+    noise = spread[3 * SPREAD + 5 : 3 * SPREAD + 6, :]
+    scale = inverse_column(noise[:, :SHELLS])
     for m in range(2):
         real = model_rows(model, MODEL, 2 * m) * scale
         imag = model_rows(model, MODEL, 2 * m + 1) * scale
@@ -180,8 +222,8 @@
     out[rows(8, NEAR, WEIGHT), :] = jnp.broadcast_to(counts, (NEAR, LANES))
 
 
-def sums_kernel(place, spread, model, weight, out):
-    leading = place[3] == 0
+def sums_kernel(spread, model, weight, out, power_out):
+    leading = place()[3] == 0
     counts = jnp.sum(weight[rows(8, NEAR, WEIGHT), :], axis=0, keepdims=True)
     residual = jnp.zeros((SHELLS, LANES), jnp.float32)
     for m in range(2):
@@ -218,37 +260,36 @@
                 out[start : start + 8, :] = value[far * 8 : far * 8 + 8]
     power = dot(jnp.ones((8, LANES), jnp.float32), residual, ((1,), (1,)))
     power = jnp.concatenate([power, jnp.zeros_like(power)], axis=1)
+    power_out[...] = jnp.broadcast_to(power[:1], (NEAR, LANES))
     for far in range(FAR):
         start = far * SUMS + 32
         out[start : start + 1, :] = counts
-        out[start + 1 : start + 2, :] = power[:1]
-
-
-def average_kernel(sums, averages, spread_averages, residual):
+
+
+def average_kernel(sums, power, averages, spread_averages):
     total = sums[0:SUMS, :]
     for far in range(1, FAR):
         total = total + sums[far * SUMS : (far + 1) * SUMS, :]
     block = total[:32] / (total[32:33] + 1.0)
     averages[...] = block
+    residual = jnp.sum(power[...], axis=0, keepdims=True)
     for far in range(FAR):
-        spread_averages[far * 32 : far * 32 + 32, :] = block
-    residual[...] = jnp.broadcast_to(total[33:34], (NEAR, LANES))
-
-
-def next_kernel(place, spread, averages, model, residual, out, noise_out):
-    leading = place[3] == 0
-    noise = jnp.sum(residual[...], axis=0, keepdims=True)[:, :SHELLS]
+        spread_averages[far * NEXT : far * NEXT + 32, :] = block
+        spread_averages[far * NEXT + 32 : far * NEXT + 33, :] = residual
+
+
+def next_kernel(spread, averages, model, out, noise_out):
+    leading = place()[3] == 0
+    noise = jnp.sum(model[rows(32, FAR, NEXT), :], axis=0, keepdims=True)[:, :SHELLS]
     noise = noise / (PARTICLES * ANGLES)
     noise_out[...] = noise
-    row = lax.broadcasted_iota(jnp.int32, (SHELLS, SHELLS), 0)
-    column = lax.broadcasted_iota(jnp.int32, (SHELLS, SHELLS), 1)
-    scale = 1.0 / jnp.sum(jnp.where(row == column, noise, 0.0), axis=1, keepdims=True)
+    scale = inverse_column(noise)
     half_norm = jnp.zeros((SHELLS, LANES), jnp.float32)
     for m in range(2):
         packed = jnp.logical_and(leading, m == 0)
         share = jnp.where(packed, 0.5, 1.0) / ANGLES
-        real = model_rows(model, 32, 2 * m)
-        imag = model_rows(model, 32, 2 * m + 1)
+        real = model_rows(model, NEXT, 2 * m)
+        imag = model_rows(model, NEXT, 2 * m + 1)
         half_norm = half_norm + share * scale * (real * real + imag * imag)
         cross = cross_rows(particle_rows(spread, m), real * scale, imag * scale, packed)
         store_cross(out, FINAL, m, cross)
@@ -262,8 +303,8 @@
             out[rows((side * 4 + c) * FINAL + 9, 8, 8 * FINAL), :] = piece
 
 
-def evidence_kernel(place, final, inverse, averages, evidence):
-    quarter, half = place[0], place[1]
+def evidence_kernel(final, inverse, averages, evidence):
+    quarter, half, _, _ = place()
     half_norm = jnp.sum(final[rows(8, NEAR, FINAL), :], axis=0, keepdims=True)
     lane = lax.broadcasted_iota(jnp.int32, (1, LANES), 1)
     found = jnp.zeros((1, LANES), jnp.float32)
@@ -272,7 +313,7 @@
         total = peak + jnp.log(whole(jnp.sum, jnp.exp(scores - peak)))
         total = total - jnp.log(jnp.full((1, 1), CLASSES * ANGLES, jnp.float32))
         found = found + jnp.where(lane == quarter * OWN_PARTICLES + i, total, 0.0)
-    evidence[...] = found
+    evidence[...] = found[:, :8]
     packed = final[rows(9, NEAR, FINAL), :]
     pieces = []
     for part in range(2):
@@ -284,20 +325,20 @@
     averages[...] = dot(table, spectrum).T
 
 
-SMEM = pl.BlockSpec(memory_space=pltpu.SMEM)
 VMEM = pl.BlockSpec(memory_space=pltpu.VMEM)
-
-
-def call(kernel, shapes, *operands, scalars=0):
+HBM = pl.BlockSpec(memory_space=pltpu.HBM)
+
+
+def call(kernel, shapes, in_specs, *operands, scratch=(), limit=32 * 1024):
     outs = [jax.ShapeDtypeStruct(shape, jnp.float32) for shape in shapes]
-    result = pl.pallas_call(
+    return pl.pallas_call(
         kernel,
-        out_shape=outs if len(outs) > 1 else outs[0],
-        in_specs=[SMEM] * scalars + [VMEM] * (len(operands) - scalars),
-        out_specs=[VMEM] * len(outs) if len(outs) > 1 else VMEM,
-        compiler_params=pltpu.CompilerParams(vmem_limit_bytes=32 * 1024 * 1024),
+        out_shape=outs,
+        in_specs=in_specs,
+        out_specs=[VMEM] * len(outs),
+        scratch_shapes=scratch,
+        compiler_params=pltpu.CompilerParams(vmem_limit_bytes=limit * 1024),
     )(*operands)
-    return result
 
 
 def exchange(value, axes, count):
@@ -308,82 +349,91 @@
 
 def shards(particles, references, noise_var):
     forward, inverse = angle_tables()
-    near, hx, cls = (lax.axis_index(name) for name in GROUP)
-    far = lax.axis_index("far")
-    shell = far * 8 + near * 4 + hx // 2
-    leader = near * 32 + hx * 4 + cls
-    place = jnp.stack([cls, hx % 2, shell, leader]).astype(jnp.int32)
-    inv_noise = 1.0 / noise_var
+    noise = noise_var.reshape(1, SHELLS)
     with jax.named_scope("spread"):
-        spread = call(
+        (spread,) = call(
             spread_kernel,
             [(NEAR * SPREAD, LANES)],
-            place,
-            inv_noise,
+            [HBM] * 4,
+            noise,
             forward,
             particles,
             references,
-            scalars=2,
+            scratch=[
+                pltpu.VMEM((1, SHELLS), jnp.float32),
+                pltpu.VMEM((ANGLES, ANGLES), jnp.float32),
+                pltpu.VMEM((OWN_PARTICLES, SHELLS, ANGLES), jnp.float32),
+                pltpu.VMEM((OWN_CLASSES, HALF), jnp.float32),
+                pltpu.SemaphoreType.DMA((8,)),
+            ],
+            limit=60 * 1024,
         )
         spread = exchange(spread, GROUP, NEAR)
     with jax.named_scope("model"):
-        model = call(model_kernel, [(FAR * MODEL, LANES)], spread)
+        (model,) = call(model_kernel, [(FAR * MODEL, LANES)], [VMEM], spread)
         model = exchange(model, "far", FAR)
     with jax.named_scope("cross"):
         cross, half_norm = call(
             cross_kernel,
             [(NEAR * CROSS, LANES), (8, LANES)],
-            place,
-            inv_noise.reshape(SHELLS, 1),
+            [VMEM] * 2,
             spread,
             model,
-            scalars=1,
         )
         cross = exchange(cross, GROUP, NEAR)
     with jax.named_scope("posterior"):
-        weight = call(
-            posterior_kernel, [(NEAR * WEIGHT, LANES)], cross, half_norm, forward, inverse
+        (weight,) = call(
+            posterior_kernel,
+            [(NEAR * WEIGHT, LANES)],
+            [VMEM] * 4,
+            cross,
+            half_norm,
+            forward,
+            inverse,
         )
         weight = exchange(weight, GROUP, NEAR)
     with jax.named_scope("sums"):
-        sums = call(
-            sums_kernel, [(FAR * SUMS, LANES)], place, spread, model, weight, scalars=1
-        )
+        sums, power = call(
+            sums_kernel,
+            [(FAR * SUMS, LANES), (NEAR, LANES)],
+            [VMEM] * 3,
+            spread,
+            model,
+            weight,
+        )
+        power = exchange(power, GROUP, NEAR)
+        sums, power = lax.optimization_barrier((sums, power))
         sums = exchange(sums, "far", FAR)
     with jax.named_scope("averages"):
-        own, next_model, residual = call(
-            average_kernel, [(32, LANES), (FAR * 32, LANES), (NEAR, LANES)], sums
-        )
-        residual = exchange(residual, GROUP, NEAR)
+        own, next_model = call(
+            average_kernel, [(32, LANES), (FAR * NEXT, LANES)], [VMEM] * 2, sums, power
+        )
         next_model = exchange(next_model, "far", FAR)
     with jax.named_scope("next"):
         final, noise_new = call(
             next_kernel,
             [(NEAR * FINAL, LANES), (1, SHELLS)],
-            place,
+            [VMEM] * 3,
             spread,
             own,
             next_model,
-            residual,
-            scalars=1,
         )
         final = exchange(final, GROUP, NEAR)
     with jax.named_scope("evidence"):
         averages, evidence = call(
             evidence_kernel,
-            [(OWN_CLASSES, LANES), (1, LANES)],
-            place,
+            [(OWN_CLASSES, LANES), (1, 8)],
+            [VMEM] * 2,
             final,
             inverse,
-            scalars=1,
-        )
-        evidence = lax.psum(evidence[0, :8], "cls")
+        )
+        evidence = lax.psum(evidence.reshape(8), "cls")
     return averages, noise_new.reshape(SHELLS), evidence
 
 
 def solution(mesh):
-    split = Mesh(mesh.devices.reshape(FAR, 2, 8, 4), ("far", "near", "hx", "cls"))
-    dom = ("far", "near", "hx")
+    split = Mesh(mesh.devices.reshape(FAR, 2, 2, 4, 4), ("far", "near", "h", "x", "cls"))
+    dom = ("far", "near", "h", "x")
     return jax.shard_map(
         shards,
         mesh=split,

time: 162 us -> 156 us (0.963)
  blocking collectives: 123 us -> 148 us
  starting transfers between devices: 13.8 us -> 0 us
  waiting for transfers between devices: 13 us -> 0 us
  local copies, waits for them, and re-layouts: 2.75 us -> 0.01 us
    all_to_all x7 -> x8, blocking collectives: 116 us -> 141 us  [exchange(): got = lax.all_to_all(sent, axes, 0, 0, tiled=True)]
    all_to_all x1 -> x0, starting transfers between devices: 13.8 us -> none  [exchange(): got = lax.all_to_all(sent, axes, 0, 0, tiled=True)]
    all_to_all x1 -> x0, waiting for transfers between devices: 13 us -> none  [exchange(): got = lax.all_to_all(sent, axes, 0, 0, tiled=True)]
    unnamed x12 -> x4, local copies, waits for them, and re-layouts: 2.65 us -> 0.01 us
  transfers between devices with their start and end apart: 1 -> 0, of which waited for: 1 -> 0; matrix products, arithmetic and copies ran while one was open for 0% -> 0% of each run, Pallas kernels for 0% -> 0%
where the time goes in v2:
time: 156 us; the launch traced here: 155 us
  blocking collectives  148 us (95%)
  Pallas kernels  7 us (4%)
    all_to_all x8, blocking collectives, exchange(): got = lax.all_to_all(sent, axes, 0, 0, tiled=True)  141 us
    pallas_call x8, Pallas kernels, call(): pl.pallas_call(kernel, out_shape=outs, in_specs=in_specs, out_specs=[VMEM...  7 us
    psum x1, blocking collectives, shards(): evidence = lax.psum(evidence.reshape(8), 'cls')  6.22 us

profile of v2, /device:TPU:1, one launch (start us, length us, event | category | flops | bytes accessed | tf_op | source)
XLA Modules:
  0.0 155.4 jit_solution(1844152164822477571)
XLA Ops:
  0.6 2.4 %spread.1 = f32[384,128]{1,0:T(8,128)} custom-call(f32[1,64]{1,0:T(1,128)} %bitcast.42, f32[256,256]{1,0:T(8,128)} %constant.4.clone.table_ref.forward, f32[8,64,256]{2,1,0:T(8,128)} %particles.1, f32[32,128]{1,0:T(8,128)} %references.1), custom_call_target="tpu_custom_call" | custom-call | tf_op jit(solution)/shard_map/spread/pallas_call | solution.py:334
  3.0 20.2 %all_to_all.40 = f32[64,1,768]{2,1,0:T(1,128)S(1)} all-to-all(f32[64,1,768]{2,1,0:T(1,128)} %bitcast.41), channel_id=1, replica_groups=mesh['far'=8,'near'=2,'h'=2,'x'=4,'cls'=4] {'near','h','x','cls'}, dimensions={0} | all-to-all | bytes 393216 | tf_op jit(solution)/shard_map/spread/all_to_all | solution.py:346
  23.2 0.1 model.1
  23.3 26.1 %all_to_all.41 = f32[8,1,4224]{2,1,0:T(1,128)S(1)} all-to-all(f32[8,1,4224]{2,1,0:T(1,128)S(1)} %bitcast.33), channel_id=1, replica_groups=mesh['far'=8,'near'=2,'h'=2,'x'=4,'cls'=4] {'far'}, dimensions={0} | all-to-all | bytes 270336 | tf_op jit(solution)/shard_map/model/all_to_all | solution.py:346
  49.4 0.5 cross.1
  49.9 0.0 copy-start
  49.9 0.0 copy-start.1
  49.9 17.9 %all_to_all.42 = f32[64,1,1024]{2,1,0:T(1,128)S(1)} all-to-all(f32[64,1,1024]{2,1,0:T(1,128)S(1)} %bitcast.35), channel_id=1, replica_groups=mesh['far'=8,'near'=2,'h'=2,'x'=4,'cls'=4] {'near','h','x','cls'}, dimensions={0} | all-to-all | bytes 524288 | tf_op jit(solution)/shard_map/cross/all_to_all | solution.py:346
  67.8 0.0 copy-done
  67.8 0.0 copy-done.1
  67.8 1.4 posterior.1
  69.2 14.3 %all_to_all.43 = f32[64,1,1152]{2,1,0:T(1,128)S(1)} all-to-all(f32[64,1,1152]{2,1,0:T(1,128)S(1)} %bitcast.29), channel_id=1, replica_groups=mesh['far'=8,'near'=2,'h'=2,'x'=4,'cls'=4] {'near','h','x','cls'}, dimensions={0} | all-to-all | bytes 589824 | tf_op jit(solution)/shard_map/posterior/all_to_all | solution.py:346
  83.5 0.6 sums.1
  84.0 12.1 %all_to_all.44 = f32[64,1,128]{2,1,0:T(1,128)S(1)} all-to-all(f32[64,1,128]{2,1,0:T(1,128)S(1)} %bitcast.39), channel_id=1, replica_groups=mesh['far'=8,'near'=2,'h'=2,'x'=4,'cls'=4] {'near','h','x','cls'}, dimensions={0} | all-to-all | bytes 65536 | tf_op jit(solution)/shard_map/sums/all_to_all | solution.py:346
  96.2 15.8 %all_to_all.45 = f32[8,1,4224]{2,1,0:T(1,128)S(1)} all-to-all(f32[8,1,4224]{2,1,0:T(1,128)S(1)} %bitcast.36), channel_id=1, replica_groups=mesh['far'=8,'near'=2,'h'=2,'x'=4,'cls'=4] {'far'}, dimensions={0} | all-to-all | bytes 270336 | tf_op jit(solution)/shard_map/sums/all_to_all | solution.py:346
  112.0 17.4 %all_to_all.46 = f32[8,1,4224]{2,1,0:T(1,128)S(1)} all-to-all(f32[8,1,4224]{2,1,0:T(1,128)S(1)} %bitcast.37), channel_id=1, replica_groups=mesh['far'=8,'near'=2,'h'=2,'x'=4,'cls'=4] {'far'}, dimensions={0} | all-to-all | bytes 270336 | tf_op jit(solution)/shard_map/averages/all_to_all | solution.py:346
  129.4 0.8 next.1
  130.3 17.7 %all_to_all.47 = f32[64,1,1280]{2,1,0:T(1,128)S(1)} all-to-all(f32[64,1,1280]{2,1,0:T(1,128)S(1)} %bitcast.34), channel_id=1, replica_groups=mesh['far'=8,'near'=2,'h'=2,'x'=4,'cls'=4] {'near','h','x','cls'}, dimensions={0} | all-to-all | bytes 655360 | tf_op jit(solution)/shard_map/next/all_to_all | solution.py:346
  147.9 1.3 evidence.1
  149.2 6.2 %psum.7 = f32[8]{0:T(128)} all-reduce(f32[8]{0:T(128)S(1)} %bitcast.40), channel_id=1, replica_groups=mesh['far'=8,'near'=2,'h'=2,'x'=4,'cls'=4] {'cls'}, use_global_device_ids=true, to_apply=%region_0.0 | all-reduce | flops 8 | bytes 64 | tf_op jit(solution)/shard_map/evidence/psum | solution.py:430
  (1 shorter events, 0.0 us)
Async XLA Ops:
  49.9 17.9 %copy-start = (f32[256,256]{1,0:T(8,128)S(1)}, f32[256,256]{1,0:T(8,128)}, u32[]{:S(2)}) copy-start(f32[256,256]{1,0:T(8,128)} %constant.4.clone.table_ref.forward) | copy-start | bytes 786436
  49.9 17.9 %copy-start.1 = (f32[256,256]{1,0:T(8,128)S(1)}, f32[256,256]{1,0:T(8,128)}, u32[]{:S(2)}) copy-start(f32[256,256]{1,0:T(8,128)} %constant.5.clone.inverse) | copy-start | bytes 786436

commit v3 on v2

--- a/solution.py
+++ b/solution.py
@@ -17,6 +17,15 @@
 OWN_PARTICLES = 2
 PARTICLES = 1024
 LANES = 128
+FAR_ORDER = [0, 4, 2, 6, 5, 1, 7, 3]
+NEAR_ORDER = [
+    24, 14, 51, 30, 26, 3, 25, 8, 0, 42, 54, 10, 63, 55, 45, 43,
+    7, 52, 12, 38, 58, 48, 1, 28, 31, 15, 40, 60, 41, 4, 53, 36,
+    11, 35, 20, 19, 46, 34, 17, 44, 9, 50, 39, 61, 21, 13, 5, 27,
+    2, 18, 23, 56, 47, 37, 6, 29, 49, 16, 33, 57, 62, 32, 22, 59,
+]
+FAR_AT = [FAR_ORDER.index(i) for i in range(FAR)]
+NEAR_AT = [NEAR_ORDER.index(i) for i in range(NEAR)]
 
 
 def dot(left, right, contract=((1,), (0,))):
@@ -125,16 +134,25 @@
 
 
 def model_kernel(spread, out):
+    def sent(shell, side, c, row):
+        start = NEAR_AT[shell * 8 + side * 4 + c] * SPREAD + row
+        return spread[start : start + 1, :]
+
     by_class = []
+    power = jnp.zeros((1, LANES), jnp.float32)
+    lane = lax.broadcasted_iota(jnp.int32, (1, LANES), 1)
     for c in range(4):
-        first = spread[rows(c * SPREAD + 4, 8, 8 * SPREAD), :]
-        second = spread[rows((c + 4) * SPREAD + 4, 8, 8 * SPREAD), :]
-        by_class.append(first + second)
-    power = spread[rows(5, NEAR, SPREAD), :]
-    lane = lax.broadcasted_iota(jnp.int32, power.shape, 1)
-    sender = lax.broadcasted_iota(jnp.int32, power.shape, 0)
-    own = lax.shift_right_logical(lane, 5) == lax.bitwise_and(sender, 3)
-    power = jnp.sum(jnp.where(own, power, 0.0), axis=0, keepdims=True)
+        models, powers = [], []
+        for side in range(2):
+            models.append(
+                jnp.concatenate([sent(shell, side, c, 4) for shell in range(8)], axis=0)
+            )
+            powers.append(
+                jnp.concatenate([sent(shell, side, c, 5) for shell in range(8)], axis=0)
+            )
+        by_class.append(models[0] + models[1])
+        total = jnp.sum(powers[0] + powers[1], axis=0, keepdims=True)
+        power = power + jnp.where(lane // OWN_CLASSES == c, total, 0.0)
     pieces = []
     for j in range(4):
         span = slice(j * OWN_CLASSES, (j + 1) * OWN_CLASSES)
@@ -147,7 +165,7 @@
 
 def model_rows(model, stride, j):
     return jnp.concatenate(
-        [model[far * stride + j * 8 : far * stride + j * 8 + 8, :] for far in range(FAR)],
+        [model[at * stride + j * 8 : at * stride + j * 8 + 8, :] for at in FAR_AT],
         axis=0,
     )
 
@@ -174,8 +192,9 @@
 
 
 def cross_kernel(spread, model, out, half_norm):
-    leading = place()[3] == 0
-    noise = spread[3 * SPREAD + 5 : 3 * SPREAD + 6, :]
+    leading = place()[3] == NEAR_ORDER[0]
+    start = NEAR_AT[3] * SPREAD + 5
+    noise = spread[start : start + 1, :]
     scale = inverse_column(noise[:, :SHELLS])
     for m in range(2):
         real = model_rows(model, MODEL, 2 * m) * scale
@@ -223,7 +242,7 @@
 
 
 def sums_kernel(spread, model, weight, out, power_out):
-    leading = place()[3] == 0
+    leading = place()[3] == NEAR_ORDER[0]
     counts = jnp.sum(weight[rows(8, NEAR, WEIGHT), :], axis=0, keepdims=True)
     residual = jnp.zeros((SHELLS, LANES), jnp.float32)
     for m in range(2):
@@ -256,7 +275,7 @@
             ref = model_rows(model, MODEL, j)
             residual = residual + share * ref * (counts * ref - 2.0 * value)
             for far in range(FAR):
-                start = far * SUMS + j * 8
+                start = FAR_AT[far] * SUMS + j * 8
                 out[start : start + 8, :] = value[far * 8 : far * 8 + 8]
     power = dot(jnp.ones((8, LANES), jnp.float32), residual, ((1,), (1,)))
     power = jnp.concatenate([power, jnp.zeros_like(power)], axis=1)
@@ -279,7 +298,7 @@
 
 
 def next_kernel(spread, averages, model, out, noise_out):
-    leading = place()[3] == 0
+    leading = place()[3] == NEAR_ORDER[0]
     noise = jnp.sum(model[rows(32, FAR, NEXT), :], axis=0, keepdims=True)[:, :SHELLS]
     noise = noise / (PARTICLES * ANGLES)
     noise_out[...] = noise
@@ -300,7 +319,9 @@
         span = slice(c * OWN_CLASSES, (c + 1) * OWN_CLASSES)
         piece = jnp.concatenate([part[:, span] for part in own], axis=1)
         for side in range(2):
-            out[rows((side * 4 + c) * FINAL + 9, 8, 8 * FINAL), :] = piece
+            for shell in range(8):
+                start = NEAR_AT[shell * 8 + side * 4 + c] * FINAL + 9
+                out[start : start + 1, :] = piece[shell : shell + 1]
 
 
 def evidence_kernel(final, inverse, averages, evidence):
@@ -341,9 +362,9 @@
     )(*operands)
 
 
-def exchange(value, axes, count):
-    sent = value.reshape(count, 1, value.size // count)
-    got = lax.all_to_all(sent, axes, 0, 0, tiled=True)
+def exchange(value, axes, order):
+    sent = value.reshape(len(order), 1, value.size // len(order))
+    got = lax.all_to_all(sent, axes, 0, 0, tiled=True, axis_index_groups=[order])
     return got.reshape(value.shape)
 
 
@@ -368,10 +389,10 @@
             ],
             limit=60 * 1024,
         )
-        spread = exchange(spread, GROUP, NEAR)
+        spread = exchange(spread, GROUP, NEAR_ORDER)
     with jax.named_scope("model"):
         (model,) = call(model_kernel, [(FAR * MODEL, LANES)], [VMEM], spread)
-        model = exchange(model, "far", FAR)
+        model = exchange(model, "far", FAR_ORDER)
     with jax.named_scope("cross"):
         cross, half_norm = call(
             cross_kernel,
@@ -380,7 +401,7 @@
             spread,
             model,
         )
-        cross = exchange(cross, GROUP, NEAR)
+        cross = exchange(cross, GROUP, NEAR_ORDER)
     with jax.named_scope("posterior"):
         (weight,) = call(
             posterior_kernel,
@@ -391,7 +412,7 @@
             forward,
             inverse,
         )
-        weight = exchange(weight, GROUP, NEAR)
+        weight = exchange(weight, GROUP, NEAR_ORDER)
     with jax.named_scope("sums"):
         sums, power = call(
             sums_kernel,
@@ -401,14 +422,14 @@
             model,
             weight,
         )
-        power = exchange(power, GROUP, NEAR)
+        power = exchange(power, GROUP, NEAR_ORDER)
         sums, power = lax.optimization_barrier((sums, power))
-        sums = exchange(sums, "far", FAR)
+        sums = exchange(sums, "far", FAR_ORDER)
     with jax.named_scope("averages"):
         own, next_model = call(
             average_kernel, [(32, LANES), (FAR * NEXT, LANES)], [VMEM] * 2, sums, power
         )
-        next_model = exchange(next_model, "far", FAR)
+        next_model = exchange(next_model, "far", FAR_ORDER)
     with jax.named_scope("next"):
         final, noise_new = call(
             next_kernel,
@@ -418,7 +439,7 @@
             own,
             next_model,
         )
-        final = exchange(final, GROUP, NEAR)
+        final = exchange(final, GROUP, NEAR_ORDER)
     with jax.named_scope("evidence"):
         averages, evidence = call(
             evidence_kernel,

time: 156 us -> 150 us (0.962)
  blocking collectives: 148 us -> 141 us
    all_to_all x8, blocking collectives: 141 us -> 135 us  [exchange(): lax.all_to_all(sent, axes, 0, 0, tiled=True, axis_index_groups=[order])]
where the time goes in v3:
time: 150 us; the launch traced here: 149 us
  blocking collectives  141 us (94%)
  Pallas kernels  7.04 us (5%)
    all_to_all x8, blocking collectives, exchange(): lax.all_to_all(sent, axes, 0, 0, tiled=True, axis_index_groups=[order])  135 us
    pallas_call x8, Pallas kernels, call(): pl.pallas_call(kernel, out_shape=outs, in_specs=in_specs, out_specs=[VMEM...  7.04 us
    psum x1, blocking collectives, shards(): evidence = lax.psum(evidence.reshape(8), 'cls')  6.46 us

profile of v3, /device:TPU:1, one launch (start us, length us, event | category | flops | bytes accessed | tf_op | source)
XLA Modules:
  0.0 148.7 jit_solution(9543678125244177465)
XLA Ops:
  0.6 2.4 %spread.1 = f32[384,128]{1,0:T(8,128)} custom-call(f32[1,64]{1,0:T(1,128)} %bitcast.42, f32[256,256]{1,0:T(8,128)} %constant.4.clone.table_ref.forward, f32[8,64,256]{2,1,0:T(8,128)} %particles.1, f32[32,128]{1,0:T(8,128)} %references.1), custom_call_target="tpu_custom_call" | custom-call | tf_op jit(solution)/shard_map/spread/pallas_call | solution.py:355
  3.0 18.4 %all_to_all.40 = f32[64,1,768]{2,1,0:T(1,128)S(1)} all-to-all(f32[64,1,768]{2,1,0:T(1,128)} %bitcast.41), channel_id=1, replica_groups={{24,14,51,30,26,3,25,8,0,42,54,10,63,55,45,43,7,52,12,38,58,48,1,28,31,..., dimensions={0} | all-to-all | bytes 393216 | tf_op jit(solution)/shard_map/spread/all_to_all | solution.py:367
  21.4 0.1 model.1
  21.5 23.2 %all_to_all.41 = f32[8,1,4224]{2,1,0:T(1,128)S(1)} all-to-all(f32[8,1,4224]{2,1,0:T(1,128)S(1)} %bitcast.33), channel_id=1, replica_groups={{0,256,128,384,320,64,448,192},{1,257,129,385,321,65,449,193},{2,258,13..., dimensions={0} | all-to-all | bytes 270336 | tf_op jit(solution)/shard_map/model/all_to_all | solution.py:367
  44.7 0.5 cross.1
  45.2 0.0 copy-start
  45.2 0.0 copy-start.1
  45.2 15.5 %all_to_all.42 = f32[64,1,1024]{2,1,0:T(1,128)S(1)} all-to-all(f32[64,1,1024]{2,1,0:T(1,128)S(1)} %bitcast.35), channel_id=1, replica_groups={{24,14,51,30,26,3,25,8,0,42,54,10,63,55,45,43,7,52,12,38,58,48,1,28,31,..., dimensions={0} | all-to-all | bytes 524288 | tf_op jit(solution)/shard_map/cross/all_to_all | solution.py:367
  60.7 0.0 copy-done
  60.7 0.0 copy-done.1
  60.7 1.4 posterior.1
  62.1 14.2 %all_to_all.43 = f32[64,1,1152]{2,1,0:T(1,128)S(1)} all-to-all(f32[64,1,1152]{2,1,0:T(1,128)S(1)} %bitcast.29), channel_id=1, replica_groups={{24,14,51,30,26,3,25,8,0,42,54,10,63,55,45,43,7,52,12,38,58,48,1,28,31,..., dimensions={0} | all-to-all | bytes 589824 | tf_op jit(solution)/shard_map/posterior/all_to_all | solution.py:367
  76.3 0.6 sums.1
  76.9 12.6 %all_to_all.44 = f32[64,1,128]{2,1,0:T(1,128)S(1)} all-to-all(f32[64,1,128]{2,1,0:T(1,128)S(1)} %bitcast.39), channel_id=1, replica_groups={{24,14,51,30,26,3,25,8,0,42,54,10,63,55,45,43,7,52,12,38,58,48,1,28,31,..., dimensions={0} | all-to-all | bytes 65536 | tf_op jit(solution)/shard_map/sums/all_to_all | solution.py:367
  89.4 16.3 %all_to_all.45 = f32[8,1,4224]{2,1,0:T(1,128)S(1)} all-to-all(f32[8,1,4224]{2,1,0:T(1,128)S(1)} %bitcast.36), channel_id=1, replica_groups={{0,256,128,384,320,64,448,192},{1,257,129,385,321,65,449,193},{2,258,13..., dimensions={0} | all-to-all | bytes 270336 | tf_op jit(solution)/shard_map/sums/all_to_all | solution.py:367
  105.8 18.1 %all_to_all.46 = f32[8,1,4224]{2,1,0:T(1,128)S(1)} all-to-all(f32[8,1,4224]{2,1,0:T(1,128)S(1)} %bitcast.37), channel_id=1, replica_groups={{0,256,128,384,320,64,448,192},{1,257,129,385,321,65,449,193},{2,258,13..., dimensions={0} | all-to-all | bytes 270336 | tf_op jit(solution)/shard_map/averages/all_to_all | solution.py:367
  123.9 0.8 next.1
  124.8 16.3 %all_to_all.47 = f32[64,1,1280]{2,1,0:T(1,128)S(1)} all-to-all(f32[64,1,1280]{2,1,0:T(1,128)S(1)} %bitcast.34), channel_id=1, replica_groups={{24,14,51,30,26,3,25,8,0,42,54,10,63,55,45,43,7,52,12,38,58,48,1,28,31,..., dimensions={0} | all-to-all | bytes 655360 | tf_op jit(solution)/shard_map/next/all_to_all | solution.py:367
  141.0 1.3 evidence.1
  142.3 6.5 %psum.7 = f32[8]{0:T(128)} all-reduce(f32[8]{0:T(128)S(1)} %bitcast.40), channel_id=1, replica_groups=mesh['far'=8,'near'=2,'h'=2,'x'=4,'cls'=4] {'cls'}, use_global_device_ids=true, to_apply=%region_0.0 | all-reduce | flops 8 | bytes 64 | tf_op jit(solution)/shard_map/evidence/psum | solution.py:451
  (1 shorter events, 0.0 us)
Async XLA Ops:
  45.2 15.5 %copy-start = (f32[256,256]{1,0:T(8,128)S(1)}, f32[256,256]{1,0:T(8,128)}, u32[]{:S(2)}) copy-start(f32[256,256]{1,0:T(8,128)} %constant.4.clone.table_ref.forward) | copy-start | bytes 786436
  45.2 15.5 %copy-start.1 = (f32[256,256]{1,0:T(8,128)S(1)}, f32[256,256]{1,0:T(8,128)}, u32[]{:S(2)}) copy-start(f32[256,256]{1,0:T(8,128)} %constant.5.clone.inverse) | copy-start | bytes 786436

commit v4 on v3

--- a/solution.py
+++ b/solution.py
@@ -19,10 +19,10 @@
 LANES = 128
 FAR_ORDER = [0, 4, 2, 6, 5, 1, 7, 3]
 NEAR_ORDER = [
-    24, 14, 51, 30, 26, 3, 25, 8, 0, 42, 54, 10, 63, 55, 45, 43,
-    7, 52, 12, 38, 58, 48, 1, 28, 31, 15, 40, 60, 41, 4, 53, 36,
-    11, 35, 20, 19, 46, 34, 17, 44, 9, 50, 39, 61, 21, 13, 5, 27,
-    2, 18, 23, 56, 47, 37, 6, 29, 49, 16, 33, 57, 62, 32, 22, 59,
+    27, 33, 58, 22, 8, 32, 48, 57, 23, 10, 15, 11, 50, 61, 52, 1,
+    28, 6, 37, 41, 20, 31, 43, 59, 53, 4, 3, 2, 38, 26, 14, 42,
+    63, 17, 45, 44, 60, 47, 55, 12, 16, 5, 35, 25, 21, 19, 34, 24,
+    40, 62, 9, 39, 13, 46, 51, 56, 54, 0, 49, 29, 7, 36, 18, 30,
 ]
 FAR_AT = [FAR_ORDER.index(i) for i in range(FAR)]
 NEAR_AT = [NEAR_ORDER.index(i) for i in range(NEAR)]

time: 150 us -> 148 us (0.987)
  blocking collectives: 141 us -> 139 us
    all_to_all x8, blocking collectives: 135 us -> 133 us  [exchange(): lax.all_to_all(sent, axes, 0, 0, tiled=True, axis_index_groups=[order])]
where the time goes in v4:
time: 148 us; the launch traced here: 147 us
  blocking collectives  139 us (94%)
  Pallas kernels  7.04 us (5%)
    all_to_all x8, blocking collectives, exchange(): lax.all_to_all(sent, axes, 0, 0, tiled=True, axis_index_groups=[order])  133 us
    pallas_call x8, Pallas kernels, call(): pl.pallas_call(kernel, out_shape=outs, in_specs=in_specs, out_specs=[VMEM...  7.04 us
    psum x1, blocking collectives, shards(): evidence = lax.psum(evidence.reshape(8), 'cls')  5.89 us

profile of v4, /device:TPU:1, one launch (start us, length us, event | category | flops | bytes accessed | tf_op | source)
XLA Modules:
  0.0 146.6 jit_solution(10202958212386704408)
XLA Ops:
  0.6 2.4 %spread.1 = f32[384,128]{1,0:T(8,128)} custom-call(f32[1,64]{1,0:T(1,128)} %bitcast.42, f32[256,256]{1,0:T(8,128)} %constant.4.clone.table_ref.forward, f32[8,64,256]{2,1,0:T(8,128)} %particles.1, f32[32,128]{1,0:T(8,128)} %references.1), custom_call_target="tpu_custom_call" | custom-call | tf_op jit(solution)/shard_map/spread/pallas_call | solution.py:355
  3.0 18.6 %all_to_all.40 = f32[64,1,768]{2,1,0:T(1,128)S(1)} all-to-all(f32[64,1,768]{2,1,0:T(1,128)} %bitcast.41), channel_id=1, replica_groups={{27,33,58,22,8,32,48,57,23,10,15,11,50,61,52,1,28,6,37,41,20,31,43,59,5..., dimensions={0} | all-to-all | bytes 393216 | tf_op jit(solution)/shard_map/spread/all_to_all | solution.py:367
  21.6 0.1 model.1
  21.7 23.1 %all_to_all.41 = f32[8,1,4224]{2,1,0:T(1,128)S(1)} all-to-all(f32[8,1,4224]{2,1,0:T(1,128)S(1)} %bitcast.33), channel_id=1, replica_groups={{0,256,128,384,320,64,448,192},{1,257,129,385,321,65,449,193},{2,258,13..., dimensions={0} | all-to-all | bytes 270336 | tf_op jit(solution)/shard_map/model/all_to_all | solution.py:367
  44.9 0.5 cross.1
  45.3 0.0 copy-start
  45.3 0.0 copy-start.1
  45.4 15.6 %all_to_all.42 = f32[64,1,1024]{2,1,0:T(1,128)S(1)} all-to-all(f32[64,1,1024]{2,1,0:T(1,128)S(1)} %bitcast.35), channel_id=1, replica_groups={{27,33,58,22,8,32,48,57,23,10,15,11,50,61,52,1,28,6,37,41,20,31,43,59,5..., dimensions={0} | all-to-all | bytes 524288 | tf_op jit(solution)/shard_map/cross/all_to_all | solution.py:367
  60.9 0.0 copy-done
  60.9 0.0 copy-done.1
  60.9 1.4 posterior.1
  62.3 13.6 %all_to_all.43 = f32[64,1,1152]{2,1,0:T(1,128)S(1)} all-to-all(f32[64,1,1152]{2,1,0:T(1,128)S(1)} %bitcast.29), channel_id=1, replica_groups={{27,33,58,22,8,32,48,57,23,10,15,11,50,61,52,1,28,6,37,41,20,31,43,59,5..., dimensions={0} | all-to-all | bytes 589824 | tf_op jit(solution)/shard_map/posterior/all_to_all | solution.py:367
  75.9 0.6 sums.1
  76.4 11.7 %all_to_all.44 = f32[64,1,128]{2,1,0:T(1,128)S(1)} all-to-all(f32[64,1,128]{2,1,0:T(1,128)S(1)} %bitcast.39), channel_id=1, replica_groups={{27,33,58,22,8,32,48,57,23,10,15,11,50,61,52,1,28,6,37,41,20,31,43,59,5..., dimensions={0} | all-to-all | bytes 65536 | tf_op jit(solution)/shard_map/sums/all_to_all | solution.py:367
  88.1 16.4 %all_to_all.45 = f32[8,1,4224]{2,1,0:T(1,128)S(1)} all-to-all(f32[8,1,4224]{2,1,0:T(1,128)S(1)} %bitcast.36), channel_id=1, replica_groups={{0,256,128,384,320,64,448,192},{1,257,129,385,321,65,449,193},{2,258,13..., dimensions={0} | all-to-all | bytes 270336 | tf_op jit(solution)/shard_map/sums/all_to_all | solution.py:367
  104.5 18.1 %all_to_all.46 = f32[8,1,4224]{2,1,0:T(1,128)S(1)} all-to-all(f32[8,1,4224]{2,1,0:T(1,128)S(1)} %bitcast.37), channel_id=1, replica_groups={{0,256,128,384,320,64,448,192},{1,257,129,385,321,65,449,193},{2,258,13..., dimensions={0} | all-to-all | bytes 270336 | tf_op jit(solution)/shard_map/averages/all_to_all | solution.py:367
  122.7 0.8 next.1
  123.5 16.0 %all_to_all.47 = f32[64,1,1280]{2,1,0:T(1,128)S(1)} all-to-all(f32[64,1,1280]{2,1,0:T(1,128)S(1)} %bitcast.34), channel_id=1, replica_groups={{27,33,58,22,8,32,48,57,23,10,15,11,50,61,52,1,28,6,37,41,20,31,43,59,5..., dimensions={0} | all-to-all | bytes 655360 | tf_op jit(solution)/shard_map/next/all_to_all | solution.py:367
  139.5 1.3 evidence.1
  140.8 5.9 %psum.7 = f32[8]{0:T(128)} all-reduce(f32[8]{0:T(128)S(1)} %bitcast.40), channel_id=1, replica_groups=mesh['far'=8,'near'=2,'h'=2,'x'=4,'cls'=4] {'cls'}, use_global_device_ids=true, to_apply=%region_0.0 | all-reduce | flops 8 | bytes 64 | tf_op jit(solution)/shard_map/evidence/psum | solution.py:451
  (1 shorter events, 0.0 us)
Async XLA Ops:
  45.3 15.6 %copy-start = (f32[256,256]{1,0:T(8,128)S(1)}, f32[256,256]{1,0:T(8,128)}, u32[]{:S(2)}) copy-start(f32[256,256]{1,0:T(8,128)} %constant.4.clone.table_ref.forward) | copy-start | bytes 786436
  45.3 15.6 %copy-start.1 = (f32[256,256]{1,0:T(8,128)S(1)}, f32[256,256]{1,0:T(8,128)}, u32[]{:S(2)}) copy-start(f32[256,256]{1,0:T(8,128)} %constant.5.clone.inverse) | copy-start | bytes 786436

commit v5 on v4

--- a/solution.py
+++ b/solution.py
@@ -17,7 +17,7 @@
 OWN_PARTICLES = 2
 PARTICLES = 1024
 LANES = 128
-FAR_ORDER = [0, 4, 2, 6, 5, 1, 7, 3]
+FAR_ORDER = [3, 1, 7, 6, 5, 2, 0, 4]
 NEAR_ORDER = [
     27, 33, 58, 22, 8, 32, 48, 57, 23, 10, 15, 11, 50, 61, 52, 1,
     28, 6, 37, 41, 20, 31, 43, 59, 53, 4, 3, 2, 38, 26, 14, 42,

time: 148 us -> 146 us (0.986)
  no operation moved by 1% of the time
where the time goes in v5:
time: 146 us
  blocking collectives  138 us (95%)
  Pallas kernels  7.02 us (5%)
    all_to_all x8, blocking collectives, exchange(): lax.all_to_all(sent, axes, 0, 0, tiled=True, axis_index_groups=[order])  132 us
    pallas_call x8, Pallas kernels, call(): pl.pallas_call(kernel, out_shape=outs, in_specs=in_specs, out_specs=[VMEM...  7.02 us
    psum x1, blocking collectives, shards(): evidence = lax.psum(evidence.reshape(8), 'cls')  5.89 us

profile of v5, /device:TPU:1, one launch (start us, length us, event | category | flops | bytes accessed | tf_op | source)
XLA Modules:
  0.0 145.6 jit_solution(7595770675524388879)
XLA Ops:
  0.6 2.4 %spread.1 = f32[384,128]{1,0:T(8,128)} custom-call(f32[1,64]{1,0:T(1,128)} %bitcast.42, f32[256,256]{1,0:T(8,128)} %constant.4.clone.table_ref.forward, f32[8,64,256]{2,1,0:T(8,128)} %particles.1, f32[32,128]{1,0:T(8,128)} %references.1), custom_call_target="tpu_custom_call" | custom-call | tf_op jit(solution)/shard_map/spread/pallas_call | solution.py:355
  3.0 18.6 %all_to_all.40 = f32[64,1,768]{2,1,0:T(1,128)S(1)} all-to-all(f32[64,1,768]{2,1,0:T(1,128)} %bitcast.41), channel_id=1, replica_groups={{27,33,58,22,8,32,48,57,23,10,15,11,50,61,52,1,28,6,37,41,20,31,43,59,5..., dimensions={0} | all-to-all | bytes 393216 | tf_op jit(solution)/shard_map/spread/all_to_all | solution.py:367
  21.6 0.1 model.1
  21.7 22.7 %all_to_all.41 = f32[8,1,4224]{2,1,0:T(1,128)S(1)} all-to-all(f32[8,1,4224]{2,1,0:T(1,128)S(1)} %bitcast.33), channel_id=1, replica_groups={{192,64,448,384,320,128,0,256},{193,65,449,385,321,129,1,257},{194,66,4..., dimensions={0} | all-to-all | bytes 270336 | tf_op jit(solution)/shard_map/model/all_to_all | solution.py:367
  44.4 0.5 cross.1
  44.9 0.0 copy-start
  44.9 0.0 copy-start.1
  44.9 15.0 %all_to_all.42 = f32[64,1,1024]{2,1,0:T(1,128)S(1)} all-to-all(f32[64,1,1024]{2,1,0:T(1,128)S(1)} %bitcast.35), channel_id=1, replica_groups={{27,33,58,22,8,32,48,57,23,10,15,11,50,61,52,1,28,6,37,41,20,31,43,59,5..., dimensions={0} | all-to-all | bytes 524288 | tf_op jit(solution)/shard_map/cross/all_to_all | solution.py:367
  59.9 0.0 copy-done
  59.9 0.0 copy-done.1
  59.9 1.4 posterior.1
  61.3 13.6 %all_to_all.43 = f32[64,1,1152]{2,1,0:T(1,128)S(1)} all-to-all(f32[64,1,1152]{2,1,0:T(1,128)S(1)} %bitcast.29), channel_id=1, replica_groups={{27,33,58,22,8,32,48,57,23,10,15,11,50,61,52,1,28,6,37,41,20,31,43,59,5..., dimensions={0} | all-to-all | bytes 589824 | tf_op jit(solution)/shard_map/posterior/all_to_all | solution.py:367
  74.8 0.6 sums.1
  75.4 11.7 %all_to_all.44 = f32[64,1,128]{2,1,0:T(1,128)S(1)} all-to-all(f32[64,1,128]{2,1,0:T(1,128)S(1)} %bitcast.39), channel_id=1, replica_groups={{27,33,58,22,8,32,48,57,23,10,15,11,50,61,52,1,28,6,37,41,20,31,43,59,5..., dimensions={0} | all-to-all | bytes 65536 | tf_op jit(solution)/shard_map/sums/all_to_all | solution.py:367
  87.1 17.1 %all_to_all.45 = f32[8,1,4224]{2,1,0:T(1,128)S(1)} all-to-all(f32[8,1,4224]{2,1,0:T(1,128)S(1)} %bitcast.36), channel_id=1, replica_groups={{192,64,448,384,320,128,0,256},{193,65,449,385,321,129,1,257},{194,66,4..., dimensions={0} | all-to-all | bytes 270336 | tf_op jit(solution)/shard_map/sums/all_to_all | solution.py:367
  104.2 18.1 %all_to_all.46 = f32[8,1,4224]{2,1,0:T(1,128)S(1)} all-to-all(f32[8,1,4224]{2,1,0:T(1,128)S(1)} %bitcast.37), channel_id=1, replica_groups={{192,64,448,384,320,128,0,256},{193,65,449,385,321,129,1,257},{194,66,4..., dimensions={0} | all-to-all | bytes 270336 | tf_op jit(solution)/shard_map/averages/all_to_all | solution.py:367
  122.3 0.8 next.1
  123.2 15.2 %all_to_all.47 = f32[64,1,1280]{2,1,0:T(1,128)S(1)} all-to-all(f32[64,1,1280]{2,1,0:T(1,128)S(1)} %bitcast.34), channel_id=1, replica_groups={{27,33,58,22,8,32,48,57,23,10,15,11,50,61,52,1,28,6,37,41,20,31,43,59,5..., dimensions={0} | all-to-all | bytes 655360 | tf_op jit(solution)/shard_map/next/all_to_all | solution.py:367
  138.4 1.3 evidence.1
  139.7 5.9 %psum.7 = f32[8]{0:T(128)} all-reduce(f32[8]{0:T(128)S(1)} %bitcast.40), channel_id=1, replica_groups=mesh['far'=8,'near'=2,'h'=2,'x'=4,'cls'=4] {'cls'}, use_global_device_ids=true, to_apply=%region_0.0 | all-reduce | flops 8 | bytes 64 | tf_op jit(solution)/shard_map/evidence/psum | solution.py:451
  (1 shorter events, 0.0 us)
Async XLA Ops:
  44.9 15.0 %copy-start = (f32[256,256]{1,0:T(8,128)S(1)}, f32[256,256]{1,0:T(8,128)}, u32[]{:S(2)}) copy-start(f32[256,256]{1,0:T(8,128)} %constant.4.clone.table_ref.forward) | copy-start | bytes 786436
  44.9 15.0 %copy-start.1 = (f32[256,256]{1,0:T(8,128)S(1)}, f32[256,256]{1,0:T(8,128)}, u32[]{:S(2)}) copy-start(f32[256,256]{1,0:T(8,128)} %constant.5.clone.inverse) | copy-start | bytes 786436
